TPU v7x, 32 devices: a whole 2x2x4 slice. The times are simulated.
32 devices in a mesh: row: 16 (over z, y, x), col: 2 (over core).
Axes of the slice: x: 2, y: 2, z: 4, core: 2. Of those that a mesh axis runs over, the one named last changes fastest.
Arguments:
- right_side: float32 [12288, 1280], P('row', 'col'), may hold values from -6 to 6
- factor_panel: bfloat16 [512, 3, 12288], P('col', None, 'row'), may hold values from -0.15625 to 0.15625
- diag_inverse: float32 [3, 512, 512], P(None, 'row'), may hold values from -1.5 to 1.5, as said below
Outputs:
- solved: float32 [12288, 1280], P('row', 'col')
Inputs may be any that keep to these rules, and one draw needn't show every extreme that they name: `diag_inverse`: each of the 3 blocks is zero above its diagonal; its diagonal lies between 0.5 and 1.5.
All inputs are finite; a program needn't handle non-finite values.
Results may differ from a plain program's by a relative error of at most 0.003.
Values may be sent and summed in bfloat16 or wider, within the bound.
A program may use at most 64 MiB of HBM per device.

v0:
```python
import jax
import jax.numpy as jnp
from jax import lax
from jax.sharding import PartitionSpec as P

KB = 3


def shards(right_side, factor_panel, diag_inverse):
    local_rows = right_side.shape[0]
    block_rows = diag_inverse.shape[1]
    workspace = right_side
    for step_index in reversed(range(KB)):
        offset = local_rows - (KB - step_index) * block_rows
        block_rhs = workspace[offset : offset + block_rows]
        partial_value = lax.dot_general(
            diag_inverse[step_index],
            block_rhs,
            (((0,), (0,)), ((), ())),
            precision=lax.Precision.HIGHEST,
            preferred_element_type=jnp.float32,
        )
        whole_x = lax.psum(partial_value, "row")
        own_rows = lax.dynamic_slice_in_dim(
            whole_x, lax.axis_index("row") * block_rows, block_rows, 0
        )
        block_low = whole_x.astype(jnp.bfloat16)
        update = lax.dot_general(
            lax.all_gather(factor_panel[:, step_index, :offset], "col", axis=0, tiled=True),
            block_low,
            (((0,), (0,)), ((), ())),
            preferred_element_type=jnp.float32,
        )
        workspace = jnp.concatenate(
            [workspace[:offset] - update, own_rows, workspace[offset + block_rows :]], axis=0
        )
    return workspace


def solution(mesh):
    placed = (P("row", "col"), P("col", None, "row"), P(None, "row", None))
    return jax.shard_map(
        shards, mesh=mesh, in_specs=placed, out_specs=P("row", "col"), check_vma=False
    )
```

profile of v0, /device:TPU:0, one launch (start us, length us, event | category | flops | bytes accessed | tf_op | source)
XLA Modules:
  0.0 380.1 jit_solution(885599477888310501)
XLA Ops:
  6.5 0.0 all-reduce.4.cloned.1.call-start
  6.5 3.2 fusion.8
  9.8 0.0 all-reduce.4.cloned.1.call-update
  9.8 0.0 all-reduce.6.cloned.1.call-start
  9.8 1.0 slice.39
  10.9 2.4 all-gather
  13.3 0.0 copy-start.2
  13.3 117.0 %all-reduce.4.cloned.1.call-done = f32[512,640]{1,0:T(8,128)} async-done(((f32[512,640]{1,0:T(8,128)}), f32[512,640]{1,0:T(8,128)}) %all-reduce.4.cloned.1.call-update) | async-done | bytes 1310736 | tf_op jit(solution)/shard_map/psum | solution.py:23
  130.3 2.7 bitcast_subtract_fusion
  133.0 0.0 copy-done.2
  133.0 2.3 convolution_bitcast_fusion.1
  135.3 0.0 all-reduce.6.cloned.1.call-update
  135.3 0.0 all-reduce.8.cloned.1.call-start
  135.4 1.0 slice.43
  136.4 2.4 all-gather.1
  138.7 111.2 %all-reduce.6.cloned.1.call-done = f32[512,640]{1,0:T(8,128)} async-done(((f32[512,640]{1,0:T(8,128)}), f32[512,640]{1,0:T(8,128)}) %all-reduce.6.cloned.1.call-update) | async-done | bytes 1310736 | tf_op jit(solution)/shard_map/psum | solution.py:23
  249.9 2.1 slice_subtract_fusion
  252.1 0.0 copy-start
  252.1 1.2 copy-done
  253.3 2.3 convolution_bitcast_fusion
  255.6 0.0 copy-start.1
  255.6 0.0 all-reduce.8.cloned.1.call-update
  255.6 1.2 slice.47
  256.8 2.4 all-gather.2
  259.1 0.9 constant_dynamic-slice_fusion
  260.1 0.9 constant_dynamic-slice_fusion.1
  261.0 108.2 %all-reduce.8.cloned.1.call-done = f32[512,640]{1,0:T(8,128)} async-done(((f32[512,640]{1,0:T(8,128)}), f32[512,640]{1,0:T(8,128)}) %all-reduce.8.cloned.1.call-update) | async-done | bytes 1310736 | tf_op jit(solution)/shard_map/psum | solution.py:23
  369.2 0.9 constant_dynamic-slice_fusion.2
  370.1 0.0 copy-done.1
  370.1 2.1 slice_subtract_fusion.1
  372.2 1.4 pad_maximum_fusion
Async XLA Ops:
  6.5 123.7 %all-reduce.4.cloned.1.call-start = ((), (), s32[]{:S(2)}) async-start(), calls=%async_computation | async-start | bytes 2621440 | tf_op jit(solution)/shard_map/psum | solution.py:23
  9.8 240.2 %all-reduce.6.cloned.1.call-start = ((), (), s32[]{:S(2)}) async-start(), calls=%async_computation.1 | async-start | bytes 2621440 | tf_op jit(solution)/shard_map/psum | solution.py:23
  13.3 119.7 %copy-start.2 = (f32[3,32,512]{2,1,0:T(8,128)S(1)}, f32[3,32,512]{2,1,0:T(8,128)}, u32[]{:S(2)}) copy-start(f32[3,32,512]{2,1,0:T(8,128)} %param.5) | copy-start | bytes 589828
  135.3 233.9 %all-reduce.8.cloned.1.call-start = ((), (), s32[]{:S(2)}) async-start(), calls=%async_computation.2 | async-start | bytes 2621440 | tf_op jit(solution)/shard_map/psum | solution.py:23
  252.1 1.2 copy-start
  255.6 114.5 %copy-start.1 = (f32[704,640]{1,0:T(8,128)S(1)}, f32[704,640]{1,0:T(8,128)}, u32[]{:S(2)}) copy-start(f32[704,640]{1,0:T(8,128)} %copy-done) | copy-start | bytes 5406724
Sparse Core Ops, SparseCore 0:
  12.8 117.4 all-reduce.3
  136.5 113.3 all-reduce.5
  255.7 113.4 all-reduce.7
where the time goes:
time: 381 us; the launch traced here: 380 us
  waiting for transfers between devices  336 us (88%)
  matrix products  14.7 us (4%)
  between operations  13.2 us (3%)
  blocking collectives  7.18 us (2%)
  local copies, waits for them, and re-layouts  7.14 us (2%)
    psum x3, waiting for transfers between devices, shards(): whole_x = lax.psum(partial_value, 'row')  336 us
    dot_general x3, matrix products, shards(): lax.dot_general(diag_inverse[step_index], block_rhs, (((0,), (0,)), ((),...  7.79 us
  transfers between devices with their start and end apart: 3, of which 3 were waited for; matrix products, arithmetic and copies ran while one was open for 1% of the time, Pallas kernels for 0%

commit v1 on v0

--- a/solution.py
+++ b/solution.py
@@ -4,6 +4,17 @@
 from jax.sharding import PartitionSpec as P
 
 KB = 3
+
+
+def numbers_name(state, which_axis):
+    n_parts = lax.axis_size(which_axis)
+    wide_out = lambda part_now: [(h, h ^ part_now) for h in range(n_parts)]
+    mid_arr = state
+    for b in range(n_parts.bit_length() - 1):
+        fresh = wide_out(1 << b)
+        w2 = lax.ppermute(mid_arr, axis_name=which_axis, perm=fresh)
+        mid_arr = mid_arr + w2
+    return mid_arr
 
 
 def shards(right_side, factor_panel, diag_inverse):
@@ -20,7 +31,7 @@
             precision=lax.Precision.HIGHEST,
             preferred_element_type=jnp.float32,
         )
-        whole_x = lax.psum(partial_value, "row")
+        whole_x = numbers_name(partial_value, "row")
         own_rows = lax.dynamic_slice_in_dim(
             whole_x, lax.axis_index("row") * block_rows, block_rows, 0
         )

time: 381 us -> 455 us (1.19)
  waiting for transfers between devices: 336 us -> 409 us
  starting transfers between devices: 0.09 us -> 23.7 us
  between operations: 13.2 us -> 0.15 us
  matrix products: 14.7 us -> 7.02 us
  local copies, waits for them, and re-layouts: 7.14 us -> 1.32 us
    ppermute x0 -> x12, waiting for transfers between devices: none -> 409 us  [numbers_name(): w2 = lax.ppermute(mid_arr, axis_name=which_axis, perm=fresh)]
    psum x3 -> x0, waiting for transfers between devices: 336 us -> none  [shards(): whole_x = lax.psum(partial_value, 'row')]
    ppermute x0 -> x12, starting transfers between devices: none -> 23.7 us  [numbers_name(): w2 = lax.ppermute(mid_arr, axis_name=which_axis, perm=fresh)]
  transfers between devices with their start and end apart: 3 -> 12, of which waited for: 3 -> 12; matrix products, arithmetic and copies ran while one was open for 1% -> 0% of each run, Pallas kernels for 0% -> 0%
where the time goes in v1:
time: 455 us; the launch traced here: 454 us
  waiting for transfers between devices  409 us (90%)
  starting transfers between devices  23.7 us (5%)
  blocking collectives  7.11 us (2%)
  matrix products  7.02 us (2%)
  other arithmetic  5.78 us (1%)
    ppermute x12, waiting for transfers between devices, numbers_name(): w2 = lax.ppermute(mid_arr, axis_name=which_axis, perm=fresh)  409 us
    ppermute x12, starting transfers between devices, numbers_name(): w2 = lax.ppermute(mid_arr, axis_name=which_axis, perm=fresh)  23.7 us
  transfers between devices with their start and end apart: 12, of which 12 were waited for; matrix products, arithmetic and copies ran while one was open for 0% of the time, Pallas kernels for 0%

profile of v1, /device:TPU:0, one launch (start us, length us, event | category | flops | bytes accessed | tf_op | source)
XLA Modules:
  0.0 454.2 jit_solution(6582658932754789972)
XLA Ops:
  0.0 2.2 fusion.8
  2.2 3.0 collective-permute-start
  5.2 28.8 %collective-permute-done = f32[512,640]{1,0:T(8,128)S(1)} collective-permute-done((f32[512,640]{1,0:T(8,128)S(1)}, f32[512,640]{1,0:T(8,128)S(1)}, u32[]{:S(2)}, u32[]{:S(2)}) %collective-permute-start) | collective-permute-done | bytes 1310752 | tf_op jit(solution)/shard_map/ppermute | solution.py:15
  34.0 0.1 add.41
  34.1 1.8 collective-permute-start.1
  35.9 28.2 %collective-permute-done.1 = f32[512,640]{1,0:T(8,128)S(1)} collective-permute-done((f32[512,640]{1,0:T(8,128)S(1)}, f32[512,640]{1,0:T(8,128)S(1)}, u32[]{:S(2)}, u32[]{:S(2)}) %collective-permute-start.1) | collective-permute-done | bytes 1310752 | tf_op jit(solution)/shard_map/ppermute | solution.py:15
  64.1 0.1 add.42
  64.3 0.0 copy-start.2
  64.3 1.6 collective-permute-start.2
  65.8 27.5 %collective-permute-done.2 = f32[512,640]{1,0:T(8,128)S(1)} collective-permute-done((f32[512,640]{1,0:T(8,128)S(1)}, f32[512,640]{1,0:T(8,128)S(1)}, u32[]{:S(2)}, u32[]{:S(2)}) %collective-permute-start.2) | collective-permute-done | bytes 1310752 | tf_op jit(solution)/shard_map/ppermute | solution.py:15
  93.4 0.1 add.43
  93.5 2.4 collective-permute-start.3
  95.9 0.0 copy-done.2
  95.9 2.4 all-gather
  98.3 0.0 copy-start.1
  98.3 52.4 %collective-permute-done.3 = f32[512,640]{1,0:T(8,128)S(1)} collective-permute-done((f32[512,640]{1,0:T(8,128)S(1)}, f32[512,640]{1,0:T(8,128)S(1)}, u32[]{:S(2)}, u32[]{:S(2)}) %collective-permute-start.3) | collective-permute-done | bytes 1310752 | tf_op jit(solution)/shard_map/ppermute | solution.py:15
  150.7 0.1 add.44
  150.8 0.0 copy-done.1
  150.8 0.0 copy-start.3
  150.8 0.8 bitcast_subtract_fusion
  151.7 0.1 copy-done.3
  151.8 1.2 convolution_bitcast_fusion.1
  153.0 0.9 collective-permute-start.4
  153.9 29.4 %collective-permute-done.4 = f32[512,640]{1,0:T(8,128)S(1)} collective-permute-done((f32[512,640]{1,0:T(8,128)S(1)}, f32[512,640]{1,0:T(8,128)S(1)}, u32[]{:S(2)}, u32[]{:S(2)}) %collective-permute-start.4) | collective-permute-done | bytes 1310752 | tf_op jit(solution)/shard_map/ppermute | solution.py:15
  183.2 0.1 add.45
  183.3 0.1 collective-permute-start.5
  183.5 29.2 %collective-permute-done.5 = f32[512,640]{1,0:T(8,128)S(1)} collective-permute-done((f32[512,640]{1,0:T(8,128)S(1)}, f32[512,640]{1,0:T(8,128)S(1)}, u32[]{:S(2)}, u32[]{:S(2)}) %collective-permute-start.5) | collective-permute-done | bytes 1310752 | tf_op jit(solution)/shard_map/ppermute | solution.py:15
  212.6 0.1 add.46
  212.8 1.2 collective-permute-start.6
  213.9 27.2 %collective-permute-done.6 = f32[512,640]{1,0:T(8,128)S(1)} collective-permute-done((f32[512,640]{1,0:T(8,128)S(1)}, f32[512,640]{1,0:T(8,128)S(1)}, u32[]{:S(2)}, u32[]{:S(2)}) %collective-permute-start.6) | collective-permute-done | bytes 1310752 | tf_op jit(solution)/shard_map/ppermute | solution.py:15
  241.1 0.1 add.47
  241.3 3.4 collective-permute-start.7
  244.7 2.4 all-gather.1
  247.1 52.2 %collective-permute-done.7 = f32[512,640]{1,0:T(8,128)S(1)} collective-permute-done((f32[512,640]{1,0:T(8,128)S(1)}, f32[512,640]{1,0:T(8,128)S(1)}, u32[]{:S(2)}, u32[]{:S(2)}) %collective-permute-start.7) | collective-permute-done | bytes 1310752 | tf_op jit(solution)/shard_map/ppermute | solution.py:15
  299.3 0.1 add.48
  299.5 0.0 copy-start
  299.5 0.8 slice_subtract_fusion
  300.3 0.2 copy-done
  300.5 1.2 convolution_bitcast_fusion
  301.8 1.6 collective-permute-start.8
  303.4 28.2 %collective-permute-done.8 = f32[512,640]{1,0:T(8,128)S(1)} collective-permute-done((f32[512,640]{1,0:T(8,128)S(1)}, f32[512,640]{1,0:T(8,128)S(1)}, u32[]{:S(2)}, u32[]{:S(2)}) %collective-permute-start.8) | collective-permute-done | bytes 1310752 | tf_op jit(solution)/shard_map/ppermute | solution.py:15
  331.6 0.1 add.49
  331.7 1.6 collective-permute-start.9
  333.3 27.3 %collective-permute-done.9 = f32[512,640]{1,0:T(8,128)S(1)} collective-permute-done((f32[512,640]{1,0:T(8,128)S(1)}, f32[512,640]{1,0:T(8,128)S(1)}, u32[]{:S(2)}, u32[]{:S(2)}) %collective-permute-start.9) | collective-permute-done | bytes 1310752 | tf_op jit(solution)/shard_map/ppermute | solution.py:15
  360.6 0.1 add.50
  360.7 2.8 collective-permute-start.10
  363.5 27.2 %collective-permute-done.10 = f32[512,640]{1,0:T(8,128)S(1)} collective-permute-done((f32[512,640]{1,0:T(8,128)S(1)}, f32[512,640]{1,0:T(8,128)S(1)}, u32[]{:S(2)}, u32[]{:S(2)}) %collective-permute-start.10) | collective-permute-done | bytes 1310752 | tf_op jit(solution)/shard_map/ppermute | solution.py:15
  390.7 1.2 add.51
  391.9 3.4 collective-permute-start.11
  395.3 2.4 all-gather.2
  397.7 0.9 constant_dynamic-slice_fusion.1
  398.6 51.6 %collective-permute-done.11 = f32[512,640]{1,0:T(8,128)} collective-permute-done((f32[512,640]{1,0:T(8,128)}, f32[512,640]{1,0:T(8,128)}, u32[]{:S(2)}, u32[]{:S(2)}) %collective-permute-start.11) | collective-permute-done | bytes 1310752 | tf_op jit(solution)/shard_map/ppermute | solution.py:15
  450.2 1.8 add.52
  452.1 0.8 slice_subtract_fusion.1
  452.8 1.4 pad_maximum_fusion
  (5 shorter events, 0.1 us)
Async XLA Ops:
  2.2 31.8 %collective-permute-start = (f32[512,640]{1,0:T(8,128)S(1)}, f32[512,640]{1,0:T(8,128)S(1)}, u32[]{:S(2)}, u32[]{:S(2)}) collective-permute-start(f32[512,640]{1,0:T(8,128)S(1)} %fusion.8), channel_id=1, source_target_pairs={{0,2},{2,0},{4,6},{6,4},{8,10},{10,8},{12,14},{14,12},{16,18},{18,... | collective-permute-start | bytes 3932168 | tf_op jit(solution)/shard_map/ppermute | solution.py:15
  34.1 30.0 %collective-permute-start.1 = (f32[512,640]{1,0:T(8,128)S(1)}, f32[512,640]{1,0:T(8,128)S(1)}, u32[]{:S(2)}, u32[]{:S(2)}) collective-permute-start(f32[512,640]{1,0:T(8,128)S(1)} %add.41), channel_id=1, source_target_pairs={{0,4},{2,6},{4,0},{6,2},{8,12},{10,14},{12,8},{14,10},{16,20},{18,... | collective-permute-start | bytes 3932168 | tf_op jit(solution)/shard_map/ppermute | solution.py:15
  64.3 31.6 %copy-start.2 = (bf16[256,3,768]{2,0,1:T(8,128)(2,1)S(1)}, bf16[256,3,768]{2,0,1:T(8,128)(2,1)}, u32[]{:S(2)}) copy-start(bf16[256,3,768]{2,0,1:T(8,128)(2,1)} %param.4) | copy-start | bytes 3538948
  64.3 29.1 %collective-permute-start.2 = (f32[512,640]{1,0:T(8,128)S(1)}, f32[512,640]{1,0:T(8,128)S(1)}, u32[]{:S(2)}, u32[]{:S(2)}) collective-permute-start(f32[512,640]{1,0:T(8,128)S(1)} %add.42), channel_id=1, source_target_pairs={{0,8},{2,10},{4,12},{6,14},{8,0},{10,2},{12,4},{14,6},{16,24},{18,... | collective-permute-start | bytes 3932168 | tf_op jit(solution)/shard_map/ppermute | solution.py:15
  93.5 57.2 %collective-permute-start.3 = (f32[512,640]{1,0:T(8,128)S(1)}, f32[512,640]{1,0:T(8,128)S(1)}, u32[]{:S(2)}, u32[]{:S(2)}) collective-permute-start(f32[512,640]{1,0:T(8,128)S(1)} %add.43), channel_id=1, source_target_pairs={{0,16},{2,18},{4,20},{6,22},{8,24},{10,26},{12,28},{14,30},{16,0},... | collective-permute-start | bytes 3932168 | tf_op jit(solution)/shard_map/ppermute | solution.py:15
  98.3 52.5 %copy-start.1 = (f32[768,640]{1,0:T(8,128)S(1)}, f32[768,640]{1,0:T(8,128)}, u32[]{:S(2)}) copy-start(f32[768,640]{1,0:T(8,128)} %param.3) | copy-start | bytes 5898244
  150.8 0.9 copy-start.3
  153.0 30.2 %collective-permute-start.4 = (f32[512,640]{1,0:T(8,128)S(1)}, f32[512,640]{1,0:T(8,128)S(1)}, u32[]{:S(2)}, u32[]{:S(2)}) collective-permute-start(f32[512,640]{1,0:T(8,128)S(1)} %convolution_bitcast_fusion.1), channel_id=1, source_target_pairs={{0,2},{2,0},{4,6},{6,4},{8,10},{10,8},{12,14},{14,12},{16,18},{18,... | collective-permute-start | bytes 3932168 | tf_op jit(solution)/shard_map/ppermute | solution.py:15
  183.3 29.3 %collective-permute-start.5 = (f32[512,640]{1,0:T(8,128)S(1)}, f32[512,640]{1,0:T(8,128)S(1)}, u32[]{:S(2)}, u32[]{:S(2)}) collective-permute-start(f32[512,640]{1,0:T(8,128)S(1)} %add.45), channel_id=1, source_target_pairs={{0,4},{2,6},{4,0},{6,2},{8,12},{10,14},{12,8},{14,10},{16,20},{18,... | collective-permute-start | bytes 3932168 | tf_op jit(solution)/shard_map/ppermute | solution.py:15
  212.8 28.4 %collective-permute-start.6 = (f32[512,640]{1,0:T(8,128)S(1)}, f32[512,640]{1,0:T(8,128)S(1)}, u32[]{:S(2)}, u32[]{:S(2)}) collective-permute-start(f32[512,640]{1,0:T(8,128)S(1)} %add.46), channel_id=1, source_target_pairs={{0,8},{2,10},{4,12},{6,14},{8,0},{10,2},{12,4},{14,6},{16,24},{18,... | collective-permute-start | bytes 3932168 | tf_op jit(solution)/shard_map/ppermute | solution.py:15
  241.3 58.1 %collective-permute-start.7 = (f32[512,640]{1,0:T(8,128)S(1)}, f32[512,640]{1,0:T(8,128)S(1)}, u32[]{:S(2)}, u32[]{:S(2)}) collective-permute-start(f32[512,640]{1,0:T(8,128)S(1)} %add.47), channel_id=1, source_target_pairs={{0,16},{2,18},{4,20},{6,22},{8,24},{10,26},{12,28},{14,30},{16,0},... | collective-permute-start | bytes 3932168 | tf_op jit(solution)/shard_map/ppermute | solution.py:15
  299.5 1.1 copy-start
  301.8 29.8 %collective-permute-start.8 = (f32[512,640]{1,0:T(8,128)S(1)}, f32[512,640]{1,0:T(8,128)S(1)}, u32[]{:S(2)}, u32[]{:S(2)}) collective-permute-start(f32[512,640]{1,0:T(8,128)S(1)} %convolution_bitcast_fusion), channel_id=1, source_target_pairs={{0,2},{2,0},{4,6},{6,4},{8,10},{10,8},{12,14},{14,12},{16,18},{18,... | collective-permute-start | bytes 3932168 | tf_op jit(solution)/shard_map/ppermute | solution.py:15
  331.7 28.9 %collective-permute-start.9 = (f32[512,640]{1,0:T(8,128)S(1)}, f32[512,640]{1,0:T(8,128)S(1)}, u32[]{:S(2)}, u32[]{:S(2)}) collective-permute-start(f32[512,640]{1,0:T(8,128)S(1)} %add.49), channel_id=1, source_target_pairs={{0,4},{2,6},{4,0},{6,2},{8,12},{10,14},{12,8},{14,10},{16,20},{18,... | collective-permute-start | bytes 3932168 | tf_op jit(solution)/shard_map/ppermute | solution.py:15
  360.7 30.0 %collective-permute-start.10 = (f32[512,640]{1,0:T(8,128)S(1)}, f32[512,640]{1,0:T(8,128)S(1)}, u32[]{:S(2)}, u32[]{:S(2)}) collective-permute-start(f32[512,640]{1,0:T(8,128)S(1)} %add.50), channel_id=1, source_target_pairs={{0,8},{2,10},{4,12},{6,14},{8,0},{10,2},{12,4},{14,6},{16,24},{18,... | collective-permute-start | bytes 3932168 | tf_op jit(solution)/shard_map/ppermute | solution.py:15
  391.9 58.3 %collective-permute-start.11 = (f32[512,640]{1,0:T(8,128)}, f32[512,640]{1,0:T(8,128)}, u32[]{:S(2)}, u32[]{:S(2)}) collective-permute-start(f32[512,640]{1,0:T(8,128)} %add.51), channel_id=1, source_target_pairs={{0,16},{2,18},{4,20},{6,22},{8,24},{10,26},{12,28},{14,30},{16,0},... | collective-permute-start | bytes 3932168 | tf_op jit(solution)/shard_map/ppermute | solution.py:15
